TPU v7x, 32 devices: a whole 2x2x4 slice. The times are simulated.
32 devices in a mesh: groups: 2 (over y), hid: 8 (over z, x), row: 2 (over core).
Axes of the slice: x: 2, y: 2, z: 4, core: 2. Of those that a mesh axis runs over, the one named last changes fastest.
Arguments:
- iterate: bfloat16 [7168, 2560], P('hid', ('groups', 'row')), parts along dimension 1, may hold values from -0.06298828 to 0.06298828
Outputs:
- update: float32 [7168, 2560], P('hid', ('groups', 'row')), parts along dimension 1
There are 2 independent parts, one for each index of `groups`. A program takes and returns all parts, laid end to end along the dimension named above; each array names one. Nothing has to cross between parts.
All inputs are finite; a program needn't handle non-finite values.
Results may differ from a plain program's by a relative error of at most 0.0007.
Values may be sent and summed in bfloat16 or wider, within the bound.
A program may use at most 64 MiB of HBM per device.

v0:
```python
import math

import jax
import jax.numpy as jnp
from jax import lax
from jax.sharding import PartitionSpec as P

H = 7168


coef_a = 3.4445
coef_b = -4.775
coef_c = 2.0315
update_scale = 0.2


def swapped(shard, axis, bit):
    return lax.ppermute(shard, axis, [(i, i ^ 1 << bit) for i in range(lax.axis_size(axis))])


def body(iterate):
    half_rows = iterate.shape[1]
    full_rows = lax.all_gather(iterate, "row", axis=1, tiled=True)
    gram_tile = lax.psum_scatter(
        lax.dot_general(
            full_rows, iterate, (((0,), (0,)), ((), ())), preferred_element_type=jnp.float32
        ),
        "hid",
        scatter_dimension=0,
        tiled=True,
    ).astype(jnp.bfloat16)
    row_index = lax.axis_index("row")
    gram_cols = lax.all_gather(gram_tile, "hid", axis=0, tiled=True)
    partner_cols = swapped(gram_cols, "row", 0)
    own_rows = lax.dynamic_slice_in_dim(gram_cols, row_index * half_rows, half_rows, 0)
    other_rows = lax.dynamic_slice_in_dim(gram_cols, (1 - row_index) * half_rows, half_rows, 0)
    square = jnp.dot(gram_cols, own_rows, preferred_element_type=jnp.float32)
    square = square + jnp.dot(partner_cols, other_rows, preferred_element_type=jnp.float32)
    mixing = (coef_b * gram_cols.astype(jnp.float32) + coef_c * square).astype(jnp.bfloat16)
    product = jnp.dot(full_rows, mixing, preferred_element_type=jnp.float32)
    return update_scale * math.sqrt(H) * (coef_a * iterate.astype(jnp.float32) + product)


def solution(mesh):
    return jax.shard_map(
        body,
        mesh=mesh,
        in_specs=(P("hid", ("groups", "row")),),
        out_specs=P("hid", ("groups", "row")),
        check_vma=False,
    )
```

profile of v0, /device:TPU:0, one launch (start us, length us, event | category | flops | bytes accessed | tf_op | source)
XLA Modules:
  0.0 173.9 jit_solution(10983351838632084289)
XLA Ops:
  6.5 0.0 all-gather.3.cloned.1.call-start
  6.5 0.7 all-gather.3.cloned.1.call-update
  7.3 0.0 reduce-scatter.2.cloned.1.call-start
  7.3 15.2 %all-gather.3.cloned.1.call-done = bf16[896,1280]{1,0:T(8,128)(2,1)} async-done(((bf16[896,640]{1,0:T(8,128)(2,1)}), bf16[896,1280]{1,0:T(8,128)(2,1)}) %all-gather.3.cloned.1.call-update) | async-done | bytes 2293776 | tf_op jit(solution)/shard_map/all_gather | solution.py:23
  22.5 5.8 %fusion.14 = f32[1280,640]{1,0:T(8,128)} fusion(bf16[896,1280]{1,0:T(8,128)(2,1)} %all-gather.3.cloned.1.call-done, bf16[896,640]{1,0:T(8,128)(2,1)} %param.1), kind=kOutput, calls=%fused_computation.13 | convolution fusion | flops 1468006400 | bytes 6717440 | tf_op jit(solution)/shard_map/dot_general | solution.py:25
  28.3 0.0 copy-start
  28.3 0.0 reduce-scatter.2.cloned.1.call-update
  28.3 0.0 all-gather.5.cloned.1.call-start
  28.3 77.4 %reduce-scatter.2.cloned.1.call-done = f32[160,640]{1,0:T(8,128)} async-done(((f32[1280,640]{1,0:T(8,128)}), f32[160,640]{1,0:T(8,128)}) %reduce-scatter.2.cloned.1.call-update) | async-done | bytes 409616 | tf_op jit(solution)/shard_map/reduce_scatter | solution.py:24
  105.8 1.7 convert_element_type.13
  107.5 0.0 all-gather.5.cloned.1.call-update
  107.5 44.3 %all-gather.5.cloned.1.call-done = bf16[1280,640]{1,0:T(8,128)(2,1)} async-done(((bf16[160,640]{1,0:T(8,128)(2,1)}), bf16[1280,640]{1,0:T(8,128)(2,1)}) %all-gather.5.cloned.1.call-update) | async-done | bytes 1638416 | tf_op jit(solution)/shard_map/all_gather | solution.py:33
  151.7 0.0 collective-permute-start
  151.8 0.0 copy-done
  151.8 1.1 copy.2
  152.9 4.9 %fusion.5 = f32[1280,640]{1,0:T(8,128)} fusion(bf16[1280,640]{1,0:T(8,128)(2,1)} %all-gather.5.cloned.1.call-done, s32[]{:T(128)S(6)} %select_n.6), kind=kOutput, calls=%fused_computation.7 | convolution fusion | flops 1048576000 | bytes 5734404 | tf_op jit(solution)/shard_map/dot_general | solution.py:37
  157.8 0.0 collective-permute-done
  157.8 7.4 %fusion.3 = f32[896,640]{0,1:T(8,128)S(1)} fusion(bf16[896,640]{0,1:T(8,128)(2,1)S(1)} %copy.2, bf16[896,1280]{1,0:T(8,128)(2,1)} %all-gather.3.cloned.1.call-done, f32[1280,640]{1,0:T(8,128)} %fusion.5, bf16[1280,640]{1,0:T(8,128)(2,1)} %collective-permute-done, bf16[1280,640]{1,0:T(8,128)(2,1)} %all-gather.5.cloned.1.call-done, s32[]{:T(128)S(6)} %select_n.7), kind=kOutput, calls=%fused_computation.5 | convolution fusion | flops 2523791360 | bytes 13107204 | tf_op jit(solution)/shard_map/dot_general | solution.py:40
  165.2 2.1 %copy.3 = f32[896,640]{1,0:T(8,128)} copy(f32[896,640]{0,1:T(8,128)S(1)} %fusion.3) | data formatting | bytes 4587520 | tf_op jit(solution)/shard_map/mul | solution.py:41
Async XLA Ops:
  6.5 15.9 %all-gather.3.cloned.1.call-start = ((), (), s32[]{:S(2)}) async-start(), calls=%async_computation.1 | async-start | bytes 3440640 | tf_op jit(solution)/shard_map/all_gather | solution.py:23
  7.3 98.5 %reduce-scatter.2.cloned.1.call-start = ((), (), s32[]{:S(2)}) async-start(), calls=%async_computation.2 | async-start | bytes 3686400 | tf_op jit(solution)/shard_map/reduce_scatter | solution.py:24
  28.3 123.5 %copy-start = (bf16[896,640]{1,0:T(8,128)(2,1)S(1)}, bf16[896,640]{1,0:T(8,128)(2,1)}, u32[]{:S(2)}) copy-start(bf16[896,640]{1,0:T(8,128)(2,1)} %param.1) | copy-start | bytes 3440644
  28.3 123.5 %all-gather.5.cloned.1.call-start = ((), (), s32[]{:S(2)}) async-start(), calls=%async_computation.3 | async-start | bytes 1843200 | tf_op jit(solution)/shard_map/all_gather | solution.py:33
  151.7 6.1 %collective-permute-start = (bf16[1280,640]{1,0:T(8,128)(2,1)}, bf16[1280,640]{1,0:T(8,128)(2,1)}, u32[]{:S(2)}, u32[]{:S(2)}) collective-permute-start(bf16[1280,640]{1,0:T(8,128)(2,1)} %all-gather.5.cloned.1.call-done), channel_id=1, source_target_pairs={{0,1},{1,0},{2,3},{3,2},{4,5},{5,4},{6,7},{7,6},{8,9},{9,8},{10,11... | collective-permute-start | bytes 4915208 | tf_op jit(solution)/shard_map/ppermute | solution.py:18
Sparse Core Ops, SparseCore 0:
  8.9 13.5 all-gather.2
  28.4 77.3 reduce-scatter.1
  108.2 43.5 all-gather.4
where the time goes:
time: 174 us
  waiting for transfers between devices  138 us (79%)
  matrix products  18.1 us (10%)
  between operations  13.1 us (8%)
  local copies, waits for them, and re-layouts  3.26 us (2%)
    reduce_scatter x1, waiting for transfers between devices, body(): lax.psum_scatter(lax.dot_general(full_rows, iterate, (((0,), (0,)), ((),...  77.4 us
    all_gather x1, waiting for transfers between devices, body(): gram_cols = lax.all_gather(gram_tile, 'hid', axis=0, tiled=True)  44.3 us
    all_gather x1, waiting for transfers between devices, body(): full_rows = lax.all_gather(iterate, 'row', axis=1, tiled=True)  15.2 us
    dot_general x1, matrix products, body(): product = jnp.dot(full_rows, mixing, preferred_element_type=jnp.float32)  7.37 us
    dot_general x1, matrix products, body(): lax.dot_general(full_rows, iterate, (((0,), (0,)), ((), ())), preferred_e...  5.8 us
    dot_general x1, matrix products, body(): square = jnp.dot(gram_cols, own_rows, preferred_element_type=jnp.float32)  4.94 us
  transfers between devices with their start and end apart: 4, of which 3 were waited for; matrix products, arithmetic and copies ran while one was open for 3% of the time, Pallas kernels for 0%

commit v1 on v0

--- a/solution.py
+++ b/solution.py
@@ -3,6 +3,8 @@
 import jax
 import jax.numpy as jnp
 from jax import lax
+from jax.experimental import pallas as pl
+from jax.experimental.pallas import tpu as pltpu
 from jax.sharding import PartitionSpec as P
 
 H = 7168
@@ -12,6 +14,10 @@
 coef_b = -4.775
 coef_c = 2.0315
 update_scale = 0.2
+
+SUB = 128
+X_CHIPS = 2
+Z_CHIPS = 4
 
 
 def swapped(shard, axis, bit):
@@ -41,9 +47,187 @@
     return update_scale * math.sqrt(H) * (coef_a * iterate.astype(jnp.float32) + product)
 
 
+def aligned(value, unit=SUB):
+    return pl.multiple_of(value, unit)
+
+
+def kernel(
+    strips, x_ref, out_ref, x_all, tiles, from_x, from_z, own_g, other_g, gram, mixing,
+    x_send, x_recv, rs_x_send, rs_x_recv, rs_z_send, rs_z_recv,
+    ag_z_send, ag_z_recv, ag_x_send, ag_x_recv, core_send, core_recv,
+):
+    rows, width = x_ref.shape
+    blocks = 2 * strips
+    depth = 3 * SUB
+    half = depth // X_CHIPS
+    piece = half // Z_CHIPS
+    hid = lax.axis_index("hid")
+    core = lax.axis_index("row")
+    x, z = lax.rem(hid, X_CHIPS), lax.div(hid, X_CHIPS)
+    x_peer = {"hid": hid + 1 - 2 * x}
+    z_peers = [{"hid": lax.rem(z + d, Z_CHIPS) * X_CHIPS + x} for d in range(1, Z_CHIPS)]
+    core_peer = {"row": 1 - core}
+
+    barrier = pltpu.get_barrier_semaphore()
+    for peer in [core_peer, x_peer, *z_peers]:
+        pl.semaphore_signal(barrier, inc=1, device_id=peer, device_id_type=pl.DeviceIdType.MESH)
+    pl.semaphore_wait(barrier, 2 + len(z_peers))
+
+    def remote(src, dst, send, recv, peer):
+        return pltpu.make_async_remote_copy(
+            src_ref=src, dst_ref=dst, send_sem=send, recv_sem=recv,
+            device_id=peer, device_id_type=pl.DeviceIdType.MESH,
+        )
+
+    own_cols = pl.ds(aligned(core * width), width)
+    exchange = remote(x_ref, x_all.at[:, own_cols], x_send, x_recv, core_peer)
+    exchange.start()
+    x_all[:, own_cols] = x_ref[...]
+
+    keep = pl.multiple_of(x * half, 16)
+    give = pl.multiple_of((1 - x) * half, 16)
+    mine = pl.multiple_of(x * half + z * piece, 16)
+
+    def place(step, of_core):
+        strip = lax.rem(step + 3 * of_core, strips)
+        late = jnp.where(strip >= 3, 1, 0)
+        lower = late + of_core - 2 * late * of_core
+        return 2 * strip, 2 * strip + 3 * lower
+
+    def rs_x(s):
+        return remote(tiles.at[s, pl.ds(give, half)], from_x.at[s], rs_x_send.at[s], rs_x_recv.at[s], x_peer)
+
+    def rs_z(s, d):
+        there = lax.rem(z + d + 1, Z_CHIPS)
+        src = tiles.at[s, pl.ds(pl.multiple_of(x * half + there * piece, 16), piece)]
+        return remote(src, from_z.at[s, d], rs_z_send.at[s, d], rs_z_recv.at[s, d], z_peers[d])
+
+    def ag_z(s, d):
+        at = own_g.at[s, pl.ds(mine, piece)]
+        return remote(at, at, ag_z_send.at[s, d], ag_z_recv.at[s, d], z_peers[d])
+
+    def ag_x(s):
+        at = own_g.at[s, pl.ds(keep, half)]
+        return remote(at, at, ag_x_send.at[s], ag_x_recv.at[s], x_peer)
+
+    def to_core(s):
+        return remote(own_g.at[s], other_g.at[s], core_send.at[s], core_recv.at[s], core_peer)
+
+    def first(s):
+        if s == 1:
+            exchange.wait()
+            x_all[:, 2 * width :] = x_all[:, : 4 * SUB]
+        col, row = place(s, core)
+        tiles[s] = lax.dot_general(
+            x_all[:, pl.ds(aligned(row * SUB), depth)],
+            x_all[:, pl.ds(aligned(col * SUB), 2 * SUB)],
+            (((0,), (0,)), ((), ())),
+            preferred_element_type=jnp.float32,
+        )
+        rs_x(s).start()
+
+    def after_rs_x(s):
+        rs_x(s).wait()
+        tiles[s, pl.ds(keep, half)] += from_x[s]
+        for d in range(Z_CHIPS - 1):
+            rs_z(s, d).start()
+
+    def after_rs_z(s):
+        for d in range(Z_CHIPS - 1):
+            rs_z(s, d).wait()
+        total = tiles[s, pl.ds(mine, piece)]
+        for d in range(Z_CHIPS - 1):
+            total += from_z[s, d]
+        own_g[s, pl.ds(mine, piece)] = total.astype(jnp.bfloat16)
+        for d in range(Z_CHIPS - 1):
+            ag_z(s, d).start()
+
+    def after_ag_z(s):
+        for d in range(Z_CHIPS - 1):
+            ag_z(s, d).wait()
+        ag_x(s).start()
+
+    def lay_out(s, held, of_core):
+        col, row = place(s, of_core)
+        for i in range(3):
+            at = lax.rem(row + i, blocks)
+            block = held[s, i * SUB : (i + 1) * SUB]
+            gram[pl.ds(aligned(at * SUB), SUB), pl.ds(aligned(col * SUB), 2 * SUB)] = block
+            gram[pl.ds(aligned(col * SUB), 2 * SUB), pl.ds(aligned(at * SUB), SUB)] = block.T
+
+    def after_ag_x(s):
+        ag_x(s).wait()
+        to_core(s).start()
+        lay_out(s, own_g, core)
+
+    def last(s):
+        to_core(s).wait()
+        lay_out(s, other_g, 1 - core)
+
+    stages = [first, after_rs_x, after_rs_z, after_ag_z, after_ag_x, last]
+    for t in range(strips + len(stages) - 1):
+        for at, stage in enumerate(stages):
+            if 0 <= t - at < strips:
+                stage(t - at)
+
+    for i in range(strips):
+        at = pl.ds(i * 2 * SUB, 2 * SUB)
+        square = jnp.dot(gram[at], gram[:, own_cols], preferred_element_type=jnp.float32)
+        mixing[at] = (coef_b * gram[at, own_cols].astype(jnp.float32) + coef_c * square).astype(jnp.bfloat16)
+    step = 128
+    for i in range(rows // step):
+        at = pl.ds(i * step, step)
+        product = jnp.dot(x_all[at, : 2 * width], mixing[...], preferred_element_type=jnp.float32)
+        out_ref[at] = update_scale * math.sqrt(H) * (coef_a * x_ref[at].astype(jnp.float32) + product)
+
+
+def fused(iterate):
+    rows, width = iterate.shape
+    full = 2 * width
+    strips = full // (2 * SUB)
+    depth = 3 * SUB
+    half = depth // X_CHIPS
+    piece = half // Z_CHIPS
+    others = Z_CHIPS - 1
+    dma = pltpu.SemaphoreType.DMA
+
+    def run(*refs):
+        kernel(strips, *refs)
+
+    return pl.pallas_call(
+        run,
+        out_shape=jax.ShapeDtypeStruct((rows, width), jnp.float32),
+        in_specs=[pl.BlockSpec(memory_space=pltpu.VMEM)],
+        out_specs=pl.BlockSpec(memory_space=pltpu.VMEM),
+        scratch_shapes=[
+            pltpu.VMEM((rows, full + 4 * SUB), jnp.bfloat16),
+            pltpu.VMEM((strips, depth, 2 * SUB), jnp.float32),
+            pltpu.VMEM((strips, half, 2 * SUB), jnp.float32),
+            pltpu.VMEM((strips, others, piece, 2 * SUB), jnp.float32),
+            pltpu.VMEM((strips, depth, 2 * SUB), jnp.bfloat16),
+            pltpu.VMEM((strips, depth, 2 * SUB), jnp.bfloat16),
+            pltpu.VMEM((full, full), jnp.bfloat16),
+            pltpu.VMEM((full, width), jnp.bfloat16),
+            dma, dma,
+            dma((strips,)), dma((strips,)),
+            dma((strips, others)), dma((strips, others)),
+            dma((strips, others)), dma((strips, others)),
+            dma((strips,)), dma((strips,)),
+            dma((strips,)), dma((strips,)),
+        ],
+        compiler_params=pltpu.CompilerParams(
+            collective_id=0, has_side_effects=True, vmem_limit_bytes=48 * 1024 * 1024
+        ),
+        cost_estimate=pl.CostEstimate(
+            flops=2 * (2 * rows + full) * full * width, bytes_accessed=6 * rows * width, transcendentals=0
+        ),
+    )(iterate)
+
+
 def solution(mesh):
+    fits = mesh.shape["hid"] == X_CHIPS * Z_CHIPS and mesh.shape["row"] == 2
     return jax.shard_map(
-        body,
+        fused if fits else body,
         mesh=mesh,
         in_specs=(P("hid", ("groups", "row")),),
         out_specs=P("hid", ("groups", "row")),

time: 174 us -> 60 us (0.34)
  waiting for transfers between devices: 138 us -> 0 us
  Pallas kernels: 0 us -> 57.1 us
  matrix products: 18.1 us -> 0 us
  between operations: 13.1 us -> 0.01 us
    reduce_scatter x1 -> x0, waiting for transfers between devices: 77.4 us -> none  [body(): lax.psum_scatter(lax.dot_general(full_rows, iterate, (((0,), (0,)), ((),...]
    all_gather x2 -> x0, waiting for transfers between devices: 59.4 us -> none  [the longest x1 44.3 us: body(): gram_cols = lax.all_gather(gram_tile, 'hid', axis=0, tiled=True)]
    pallas_call x0 -> x1, Pallas kernels: none -> 57.1 us  [fused(): pl.pallas_call(run, out_shape=jax.ShapeDtypeStruct((rows, width), jnp.flo...]
    dot_general x3 -> x0, matrix products: 18.1 us -> none  [the longest x1 7.37 us: body(): product = jnp.dot(full_rows, mixing, preferred_element_type=jnp.float32)]
    mul x1 -> x0, local copies, waits for them, and re-layouts: 2.13 us -> none  [body(): update_scale * math.sqrt(H)]
  transfers between devices with their start and end apart: 4 -> 0, of which waited for: 3 -> 0; matrix products, arithmetic and copies ran while one was open for 3% -> 0% of each run, Pallas kernels for 0% -> 0%
where the time goes in v1:
time: 60 us; the launch traced here: 59.7 us
  Pallas kernels  57.1 us (95%)
  local copies, waits for them, and re-layouts  2.64 us (4%)
    pallas_call x1, Pallas kernels, fused(): pl.pallas_call(run, out_shape=jax.ShapeDtypeStruct((rows, width), jnp.flo...  57.1 us
    unnamed x3, local copies, waits for them, and re-layouts  2.64 us

profile of v1, /device:TPU:0, one launch (start us, length us, event | category | flops | bytes accessed | tf_op | source)
XLA Modules:
  0.0 59.7 jit_solution(11764351493515589099)
XLA Ops:
  0.0 0.0 copy-start
  0.0 1.3 %copy-done = bf16[896,640]{1,0:T(8,128)(2,1)S(1)} copy-done((bf16[896,640]{1,0:T(8,128)(2,1)S(1)}, bf16[896,640]{1,0:T(8,128)(2,1)}, u32[]{:S(2)}) %copy-start) | copy-done | bytes 1146904
  1.3 57.1 %shard_map.17 = f32[896,640]{1,0:T(8,128)S(1)} custom-call(bf16[896,640]{1,0:T(8,128)(2,1)S(1)} %copy-done), custom_call_target="tpu_custom_call" | custom-call | flops 5033164800 | bytes 3440640 | tf_op jit(solution)/shard_map/pallas_call | solution.py:197
  58.3 1.4 %copy.3 = f32[896,640]{1,0:T(8,128)} copy(f32[896,640]{1,0:T(8,128)S(1)} %shard_map.17) | data formatting | bytes 4587520
Async XLA Ops:
  0.0 1.3 %copy-start = (bf16[896,640]{1,0:T(8,128)(2,1)S(1)}, bf16[896,640]{1,0:T(8,128)(2,1)}, u32[]{:S(2)}) copy-start(bf16[896,640]{1,0:T(8,128)(2,1)} %refs_0_.1) | copy-start | bytes 3440644

commit v2 on v0

--- a/solution.py
+++ b/solution.py
@@ -3,6 +3,8 @@
 import jax
 import jax.numpy as jnp
 from jax import lax
+from jax.experimental import pallas as pl
+from jax.experimental.pallas import tpu as pltpu
 from jax.sharding import PartitionSpec as P
 
 H = 7168
@@ -12,6 +14,24 @@
 coef_b = -4.775
 coef_c = 2.0315
 update_scale = 0.2
+
+SUB = 128
+X_CHIPS = 2
+Z_CHIPS = 4
+CHUNKS = (
+    (0, 0, 2, 0, 3, "xz"),
+    (1, 0, 2, 0, 3, "nxf"),
+    (2, 0, 2, 0, 3, "xfn"),
+    (3, 0, 2, 0, 3, "nxf"),
+    (4, 0, 1, 0, 3, "xnf"),
+    (4, 1, 1, 0, 2, "xnf"),
+    (4, 1, 1, 2, 1, "nxf"),
+)
+ORDER = (
+    0, 1, 0, 2, 1, 3, 0, 2, 4, 1, 3, 5, 0, 4, 6, 3, 5, 4, 2, 6, 0, 1, 5, 0, 6, 3, 2, 4, 1, 5, 6, 2,
+    3, 4, 1, 5, 6, 3, 4, 2, 6, 1, 5, 4, 1, 3, 4, 6, 2, 5, 3, 6, 2, 5,
+)
+WAYS = {"x": 2, "n": 2, "f": 2, "z": 4, "d": 8}
 
 
 def swapped(shard, axis, bit):
@@ -41,9 +61,225 @@
     return update_scale * math.sqrt(H) * (coef_a * iterate.astype(jnp.float32) + product)
 
 
+def aligned(value, unit=SUB):
+    return pl.multiple_of(value, unit)
+
+
+def stage_rows(stages, left):
+    rows = []
+    for kind in stages:
+        left //= WAYS[kind]
+        rows.append(left)
+    return rows
+
+
+def kernel(strips, x_ref, out_ref, x_all, gram, mixing, x_own, x_send, x_recv, x_sem, sends, recvs, *buffers):
+    rows, width = x_ref.shape
+    blocks = 2 * strips
+    hid = lax.axis_index("hid")
+    core = lax.axis_index("row")
+    x, z = lax.rem(hid, X_CHIPS), lax.div(hid, X_CHIPS)
+    near, far = lax.rem(z, 2), lax.div(z, 2)
+    core_peer = {"row": 1 - core}
+    place_in = {"x": x, "n": near, "f": far, "z": z, "d": hid}
+    member = {
+        "x": lambda p: z * X_CHIPS + p,
+        "n": lambda p: (far * 2 + p) * X_CHIPS + x,
+        "f": lambda p: (p * 2 + near) * X_CHIPS + x,
+        "z": lambda p: p * X_CHIPS + x,
+        "d": lambda p: p,
+    }
+    own_cols = pl.ds(aligned(core * width), width)
+    fetch = pltpu.make_async_copy(x_ref, x_own, x_sem.at[0])
+    fetch.start()
+
+    kinds = set("".join(chunk[5] for chunk in CHUNKS))
+    barrier = pltpu.get_barrier_semaphore()
+    if "d" in kinds:
+        greeted = [lax.rem(hid + d, 8) for d in range(1, 8)]
+    else:
+        greeted = [z * X_CHIPS + 1 - x] + [lax.rem(z + d, Z_CHIPS) * X_CHIPS + x for d in range(1, Z_CHIPS)]
+    for peer in [core_peer] + [{"hid": one} for one in greeted]:
+        pl.semaphore_signal(barrier, inc=1, device_id=peer, device_id_type=pl.DeviceIdType.MESH)
+    pl.semaphore_wait(barrier, 1 + len(greeted))
+
+    used = [0]
+
+    def remote(src, dst, peer):
+        at = used[0]
+        used[0] += 1
+        return pltpu.make_async_remote_copy(
+            src_ref=src, dst_ref=dst, send_sem=sends.at[at], recv_sem=recvs.at[at],
+            device_id=peer, device_id_type=pl.DeviceIdType.MESH,
+        )
+
+    exchange = pltpu.make_async_remote_copy(
+        src_ref=x_ref, dst_ref=x_all.at[:, own_cols], send_sem=x_send, recv_sem=x_recv,
+        device_id=core_peer, device_id_type=pl.DeviceIdType.MESH,
+    )
+    exchange.start()
+    fetch.wait()
+    x_all[:, own_cols] = x_own[...]
+
+    def place(step, of_core):
+        strip = lax.rem(step + 3 * of_core, strips)
+        late = jnp.where(strip >= 3, 1, 0)
+        lower = late + of_core - 2 * late * of_core
+        return 2 * strip, 2 * strip + 3 * lower
+
+    buffers = list(buffers)
+
+    def add_chunk(order, step, first_block, n_blocks, first_row, n_rows, stages):
+        depth = n_rows * SUB
+        events = []
+        tile, own_g, other_g = buffers.pop(0), buffers.pop(0), buffers.pop(0)
+        arrive = [buffers.pop(0) for _ in stages]
+        lefts = stage_rows(stages, depth)
+        starts, at = [], 0
+        for kind, left in zip(stages, lefts):
+            starts.append(at)
+            at = at + place_in[kind] * left
+
+        def span(start, n):
+            return pl.ds(pl.multiple_of(start, 16), n)
+
+        def peers_of(kind):
+            ways = WAYS[kind]
+            return [lax.rem(place_in[kind] + d, ways) for d in range(1, ways)]
+
+        sums, copies = [], []
+        for i, kind in enumerate(stages):
+            sums.append([
+                remote(tile.at[span(starts[i] + p * lefts[i], lefts[i])], arrive[i].at[d], {"hid": member[kind](p)})
+                for d, p in enumerate(peers_of(kind))
+            ])
+        for i in reversed(range(len(stages))):
+            kind = stages[i]
+            held = own_g.at[span(starts[i] + place_in[kind] * lefts[i], lefts[i])]
+            copies.append([remote(held, held, {"hid": member[kind](p)}) for p in peers_of(kind)])
+        copies.append([remote(own_g, other_g, core_peer)])
+
+        def start(group):
+            for one in group:
+                one.start()
+
+        def wait(group):
+            for one in group:
+                one.wait()
+
+        def lay_out(held, of_core):
+            col, row = place(step, of_core)
+            for i in range(n_rows):
+                at = lax.rem(row + first_row + i, blocks)
+                block = held[i * SUB : (i + 1) * SUB]
+                cols = pl.ds(aligned((col + first_block) * SUB), n_blocks * SUB)
+                gram[pl.ds(aligned(at * SUB), SUB), cols] = block
+                gram[cols, pl.ds(aligned(at * SUB), SUB)] = block.T
+
+        def first():
+            if order == second:
+                exchange.wait()
+                x_all[:, 2 * width :] = x_all[:, : 4 * SUB]
+            col, row = place(step, core)
+            tile[...] = lax.dot_general(
+                x_all[:, pl.ds(aligned((row + first_row) * SUB), depth)],
+                x_all[:, pl.ds(aligned((col + first_block) * SUB), n_blocks * SUB)],
+                (((0,), (0,)), ((), ())),
+                preferred_element_type=jnp.float32,
+            )
+            start(sums[0])
+
+        def after_sum(i):
+            wait(sums[i])
+            kind, left = stages[i], lefts[i]
+            kept = span(starts[i] + place_in[kind] * left, left)
+            total = tile[kept]
+            for d in range(WAYS[kind] - 1):
+                total += arrive[i][d]
+            if i + 1 < len(stages):
+                tile[kept] = total
+                start(sums[i + 1])
+            else:
+                own_g[kept] = total.astype(jnp.bfloat16)
+                start(copies[0])
+
+        def after_copy(i):
+            wait(copies[i])
+            if i + 1 < len(copies):
+                start(copies[i + 1])
+            if i + 2 == len(copies):
+                lay_out(own_g, core)
+            if i + 1 == len(copies):
+                lay_out(other_g, 1 - core)
+
+        events.append((first, ()))
+        for i in range(len(stages)):
+            events.append((after_sum, (i,)))
+        for i in range(len(copies)):
+            events.append((after_copy, (i,)))
+        return events
+
+    second = min(i for i, chunk in enumerate(CHUNKS) if chunk[0] > 0)
+    todo = [add_chunk(order, *chunk) for order, chunk in enumerate(CHUNKS)]
+    for chunk in ORDER:
+        run, at = todo[chunk].pop(0)
+        run(*at)
+
+    for i in range(strips):
+        at = pl.ds(i * 2 * SUB, 2 * SUB)
+        square = jnp.dot(gram[at], gram[:, own_cols], preferred_element_type=jnp.float32)
+        mixing[at] = (coef_b * gram[at, own_cols].astype(jnp.float32) + coef_c * square).astype(jnp.bfloat16)
+    step = 128
+    for i in range(rows // step):
+        at = pl.ds(i * step, step)
+        product = jnp.dot(x_all[at, : 2 * width], mixing[...], preferred_element_type=jnp.float32)
+        out_ref[at] = update_scale * math.sqrt(H) * (coef_a * x_own[at].astype(jnp.float32) + product)
+
+
+def fused(iterate):
+    rows, width = iterate.shape
+    full = 2 * width
+    strips = full // (2 * SUB)
+    buffers, copies = [], 0
+    for _, _, n_blocks, _, n_rows, stages in CHUNKS:
+        cols, depth = n_blocks * SUB, n_rows * SUB
+        buffers += [pltpu.VMEM((depth, cols), jnp.float32)] + [pltpu.VMEM((depth, cols), jnp.bfloat16)] * 2
+        for kind, left in zip(stages, stage_rows(stages, depth)):
+            buffers.append(pltpu.VMEM((WAYS[kind] - 1, left, cols), jnp.float32))
+            copies += 2 * (WAYS[kind] - 1)
+        copies += 1
+    dma = pltpu.SemaphoreType.DMA
+
+    def run(*refs):
+        kernel(strips, *refs)
+
+    return pl.pallas_call(
+        run,
+        out_shape=jax.ShapeDtypeStruct((rows, width), jnp.float32),
+        in_specs=[pl.BlockSpec(memory_space=pl.ANY)],
+        out_specs=pl.BlockSpec(memory_space=pltpu.VMEM),
+        scratch_shapes=[
+            pltpu.VMEM((rows, full + 4 * SUB), jnp.bfloat16),
+            pltpu.VMEM((full, full), jnp.bfloat16),
+            pltpu.VMEM((full, width), jnp.bfloat16),
+            pltpu.VMEM((rows, width), jnp.bfloat16),
+            dma, dma, dma((1,)),
+            dma((copies,)), dma((copies,)),
+            *buffers,
+        ],
+        compiler_params=pltpu.CompilerParams(
+            collective_id=0, has_side_effects=True, vmem_limit_bytes=48 * 1024 * 1024
+        ),
+        cost_estimate=pl.CostEstimate(
+            flops=2 * (2 * rows + full) * full * width, bytes_accessed=6 * rows * width, transcendentals=0
+        ),
+    )(iterate)
+
+
 def solution(mesh):
+    fits = mesh.shape["hid"] == X_CHIPS * Z_CHIPS and mesh.shape["row"] == 2
     return jax.shard_map(
-        body,
+        fused if fits else body,
         mesh=mesh,
         in_specs=(P("hid", ("groups", "row")),),
         out_specs=P("hid", ("groups", "row")),

time: 174 us -> 57.1 us (0.33)
  waiting for transfers between devices: 138 us -> 0 us
  Pallas kernels: 0 us -> 54.3 us
  matrix products: 18.1 us -> 0 us
  between operations: 13.1 us -> 0.01 us
    reduce_scatter x1 -> x0, waiting for transfers between devices: 77.4 us -> none  [body(): lax.psum_scatter(lax.dot_general(full_rows, iterate, (((0,), (0,)), ((),...]
    all_gather x2 -> x0, waiting for transfers between devices: 59.4 us -> none  [the longest x1 44.3 us: body(): gram_cols = lax.all_gather(gram_tile, 'hid', axis=0, tiled=True)]
    pallas_call x0 -> x1, Pallas kernels: none -> 54.3 us  [fused(): pl.pallas_call(run, out_shape=jax.ShapeDtypeStruct((rows, width), jnp.flo...]
    dot_general x3 -> x0, matrix products: 18.1 us -> none  [the longest x1 7.37 us: body(): product = jnp.dot(full_rows, mixing, preferred_element_type=jnp.float32)]
    mul x1 -> x0, local copies, waits for them, and re-layouts: 2.13 us -> none  [body(): update_scale * math.sqrt(H)]
  transfers between devices with their start and end apart: 4 -> 0, of which waited for: 3 -> 0; matrix products, arithmetic and copies ran while one was open for 3% -> 0% of each run, Pallas kernels for 0% -> 0%
where the time goes in v2:
time: 57.1 us; the launch traced here: 57 us
  Pallas kernels  54.3 us (95%)
  local copies, waits for them, and re-layouts  2.64 us (5%)
    pallas_call x1, Pallas kernels, fused(): pl.pallas_call(run, out_shape=jax.ShapeDtypeStruct((rows, width), jnp.flo...  54.3 us
    unnamed x3, local copies, waits for them, and re-layouts  2.64 us

profile of v2, /device:TPU:0, one launch (start us, length us, event | category | flops | bytes accessed | tf_op | source)
XLA Modules:
  0.0 57.0 jit_solution(13379520299804230803)
XLA Ops:
  0.0 0.0 copy-start
  0.0 1.3 %copy-done = bf16[896,640]{1,0:T(8,128)(2,1)S(1)} copy-done((bf16[896,640]{1,0:T(8,128)(2,1)S(1)}, bf16[896,640]{1,0:T(8,128)(2,1)}, u32[]{:S(2)}) %copy-start) | copy-done | bytes 1146904
  1.3 54.3 %shard_map.17 = f32[896,640]{1,0:T(8,128)S(1)} custom-call(bf16[896,640]{1,0:T(8,128)(2,1)S(1)} %copy-done), custom_call_target="tpu_custom_call" | custom-call | flops 5033164800 | bytes 3440640 | tf_op jit(solution)/shard_map/pallas_call | solution.py:256
  55.6 1.4 %copy.3 = f32[896,640]{1,0:T(8,128)} copy(f32[896,640]{1,0:T(8,128)S(1)} %shard_map.17) | data formatting | bytes 4587520
Async XLA Ops:
  0.0 1.3 %copy-start = (bf16[896,640]{1,0:T(8,128)(2,1)S(1)}, bf16[896,640]{1,0:T(8,128)(2,1)}, u32[]{:S(2)}) copy-start(bf16[896,640]{1,0:T(8,128)(2,1)} %refs_0_.1) | copy-start | bytes 3440644

commit v3 on v2

--- a/solution.py
+++ b/solution.py
@@ -19,17 +19,15 @@
 X_CHIPS = 2
 Z_CHIPS = 4
 CHUNKS = (
-    (0, 0, 2, 0, 3, "xz"),
+    (0, 0, 2, 0, 3, "xnf"),
     (1, 0, 2, 0, 3, "nxf"),
-    (2, 0, 2, 0, 3, "xfn"),
-    (3, 0, 2, 0, 3, "nxf"),
-    (4, 0, 1, 0, 3, "xnf"),
-    (4, 1, 1, 0, 2, "xnf"),
-    (4, 1, 1, 2, 1, "nxf"),
+    (2, 0, 2, 0, 3, "fxn"),
+    (3, 0, 2, 0, 3, "xfn"),
+    (4, 0, 2, 0, 3, "xnf"),
 )
 ORDER = (
-    0, 1, 0, 2, 1, 3, 0, 2, 4, 1, 3, 5, 0, 4, 6, 3, 5, 4, 2, 6, 0, 1, 5, 0, 6, 3, 2, 4, 1, 5, 6, 2,
-    3, 4, 1, 5, 6, 3, 4, 2, 6, 1, 5, 4, 1, 3, 4, 6, 2, 5, 3, 6, 2, 5,
+    0, 1, 2, 3, 4, 0, 1, 3, 4, 0, 2, 1, 3, 4, 2, 0, 1, 3, 2, 4, 0, 3, 1, 2, 4, 0, 1, 3, 2, 4, 0, 1,
+    0, 3, 1, 3, 4, 2, 4, 2,
 )
 WAYS = {"x": 2, "n": 2, "f": 2, "z": 4, "d": 8}
 
@@ -225,14 +223,16 @@
         run, at = todo[chunk].pop(0)
         run(*at)
 
-    for i in range(strips):
-        at = pl.ds(i * 2 * SUB, 2 * SUB)
+    full = 2 * width
+    step = full // 2
+    for i in range(full // step):
+        at = pl.ds(i * step, step)
         square = jnp.dot(gram[at], gram[:, own_cols], preferred_element_type=jnp.float32)
         mixing[at] = (coef_b * gram[at, own_cols].astype(jnp.float32) + coef_c * square).astype(jnp.bfloat16)
-    step = 128
+    step = rows // 2
     for i in range(rows // step):
         at = pl.ds(i * step, step)
-        product = jnp.dot(x_all[at, : 2 * width], mixing[...], preferred_element_type=jnp.float32)
+        product = jnp.dot(x_all[at, :full], mixing[...], preferred_element_type=jnp.float32)
         out_ref[at] = update_scale * math.sqrt(H) * (coef_a * x_own[at].astype(jnp.float32) + product)
 
 

time: 57.1 us -> 53 us (0.928)
  Pallas kernels: 54.3 us -> 50.2 us
    pallas_call x1, Pallas kernels: 54.3 us -> 50.2 us  [fused(): pl.pallas_call(run, out_shape=jax.ShapeDtypeStruct((rows, width), jnp.flo...]
where the time goes in v3:
time: 53 us; the launch traced here: 52.9 us
  Pallas kernels  50.2 us (95%)
  local copies, waits for them, and re-layouts  2.64 us (5%)
    pallas_call x1, Pallas kernels, fused(): pl.pallas_call(run, out_shape=jax.ShapeDtypeStruct((rows, width), jnp.flo...  50.2 us
    unnamed x3, local copies, waits for them, and re-layouts  2.64 us

profile of v3, /device:TPU:0, one launch (start us, length us, event | category | flops | bytes accessed | tf_op | source)
XLA Modules:
  0.0 52.9 jit_solution(18231624739843492318)
XLA Ops:
  0.0 0.0 copy-start
  0.0 1.3 %copy-done = bf16[896,640]{1,0:T(8,128)(2,1)S(1)} copy-done((bf16[896,640]{1,0:T(8,128)(2,1)S(1)}, bf16[896,640]{1,0:T(8,128)(2,1)}, u32[]{:S(2)}) %copy-start) | copy-done | bytes 1146904
  1.3 50.2 %shard_map.17 = f32[896,640]{1,0:T(8,128)S(1)} custom-call(bf16[896,640]{1,0:T(8,128)(2,1)S(1)} %copy-done), custom_call_target="tpu_custom_call" | custom-call | flops 5033164800 | bytes 3440640 | tf_op jit(solution)/shard_map/pallas_call | solution.py:256
  51.5 1.4 %copy.3 = f32[896,640]{1,0:T(8,128)} copy(f32[896,640]{1,0:T(8,128)S(1)} %shard_map.17) | data formatting | bytes 4587520
Async XLA Ops:
  0.0 1.3 %copy-start = (bf16[896,640]{1,0:T(8,128)(2,1)S(1)}, bf16[896,640]{1,0:T(8,128)(2,1)}, u32[]{:S(2)}) copy-start(bf16[896,640]{1,0:T(8,128)(2,1)} %refs_0_.1) | copy-start | bytes 3440644

commit v4 on v3

--- a/solution.py
+++ b/solution.py
@@ -224,12 +224,12 @@
         run(*at)
 
     full = 2 * width
-    step = full // 2
+    step = full
     for i in range(full // step):
         at = pl.ds(i * step, step)
         square = jnp.dot(gram[at], gram[:, own_cols], preferred_element_type=jnp.float32)
         mixing[at] = (coef_b * gram[at, own_cols].astype(jnp.float32) + coef_c * square).astype(jnp.bfloat16)
-    step = rows // 2
+    step = rows
     for i in range(rows // step):
         at = pl.ds(i * step, step)
         product = jnp.dot(x_all[at, :full], mixing[...], preferred_element_type=jnp.float32)

time: 53 us -> 53.1 us (level)
  no operation moved by 1% of the time
where the time goes in v4:
time: 53.1 us; the launch traced here: 53 us
  Pallas kernels  50.3 us (95%)
  local copies, waits for them, and re-layouts  2.64 us (5%)
    pallas_call x1, Pallas kernels, fused(): pl.pallas_call(run, out_shape=jax.ShapeDtypeStruct((rows, width), jnp.flo...  50.3 us
    unnamed x3, local copies, waits for them, and re-layouts  2.64 us

profile of v4, /device:TPU:0, one launch (start us, length us, event | category | flops | bytes accessed | tf_op | source)
XLA Modules:
  0.0 53.0 jit_solution(5267601731261418769)
XLA Ops:
  0.0 0.0 copy-start
  0.0 1.3 %copy-done = bf16[896,640]{1,0:T(8,128)(2,1)S(1)} copy-done((bf16[896,640]{1,0:T(8,128)(2,1)S(1)}, bf16[896,640]{1,0:T(8,128)(2,1)}, u32[]{:S(2)}) %copy-start) | copy-done | bytes 1146904
  1.3 50.3 %shard_map.17 = f32[896,640]{1,0:T(8,128)S(1)} custom-call(bf16[896,640]{1,0:T(8,128)(2,1)S(1)} %copy-done), custom_call_target="tpu_custom_call" | custom-call | flops 5033164800 | bytes 3440640 | tf_op jit(solution)/shard_map/pallas_call | solution.py:256
  51.6 1.4 %copy.3 = f32[896,640]{1,0:T(8,128)} copy(f32[896,640]{1,0:T(8,128)S(1)} %shard_map.17) | data formatting | bytes 4587520
Async XLA Ops:
  0.0 1.3 %copy-start = (bf16[896,640]{1,0:T(8,128)(2,1)S(1)}, bf16[896,640]{1,0:T(8,128)(2,1)}, u32[]{:S(2)}) copy-start(bf16[896,640]{1,0:T(8,128)(2,1)} %refs_0_.1) | copy-start | bytes 3440644
